TPU v7x, 32 devices: a whole 2x2x4 slice. The times are simulated.
32 devices in a mesh: dp: 8 (over y, x, core), expert: 4 (over z).
Axes of the slice: x: 2, y: 2, z: 4, core: 2. Of those that a mesh axis runs over, the one named last changes fastest.
Arguments:
- tokens: bfloat16 [512, 4096], P('expert', 'dp'), may hold values from -6 to 6
- expert_ids: int32 [512, 8], P('expert'), may hold values from 0 to 15, all different within a row; in each aligned block of 128 rows (0 to 127, 128 to 255, ...) at most 128 rows name the same one
- gate_prob: float32 [512, 8], P('expert'), may hold values from 0.05 to 0.35
- w_gate: bfloat16 [16, 4096, 768], P('expert', 'dp'), may hold values from -0.09375 to 0.09375
- w_up: bfloat16 [16, 4096, 768], P('expert', 'dp'), may hold values from -0.09375 to 0.09375
- w_down: bfloat16 [16, 768, 4096], P('expert', None, 'dp'), may hold values from -0.21875 to 0.21875
- grad_out: bfloat16 [512, 4096], P('expert', 'dp'), may hold values from -6 to 6
Outputs:
- mixed: bfloat16 [512, 4096], P('expert', 'dp')
- grad_tokens: bfloat16 [512, 4096], P('expert', 'dp')
- grad_gate: float32 [512, 8], P('expert')
- grad_w_gate: bfloat16 [16, 4096, 768], P('expert', 'dp')
- grad_w_up: bfloat16 [16, 4096, 768], P('expert', 'dp')
- grad_w_down: bfloat16 [16, 768, 4096], P('expert', None, 'dp')
Inputs may be any that keep to these rules, and one draw needn't show every extreme that they name: `expert_ids`: each row names 8 different experts. Within the rows of one index of expert (aligned blocks of 128 rows) no expert is named by more than 128 rows, a bound that some block reaches.
All inputs are finite; a program needn't handle non-finite values.
Results may differ from a plain program's by a relative error of at most 0.035.
Values may be sent and summed in bfloat16 or wider, within the bound.
A program may use at most 128 MiB of HBM per device.

v0:
```python
import jax
import jax.numpy as jnp
from jax import lax
from jax.sharding import PartitionSpec as P


def slot_tables(expert_ids, columns, per_device, capacity):
    flat_ids = expert_ids.reshape(-1)
    assign_count = flat_ids.shape[0]
    experts_all = columns * per_device
    onehot = (flat_ids[:, None] == jnp.arange(experts_all, dtype=jnp.int32)[None, :]).astype(
        jnp.int32
    )
    before = jnp.cumsum(onehot, axis=0) - onehot
    rank_in = jnp.sum(before * onehot, axis=1)
    slot_of = (flat_ids % per_device * columns + flat_ids // per_device) * capacity + rank_in
    slot_count = experts_all * capacity
    source = (
        jnp.full((slot_count,), assign_count, jnp.int32)
        .at[slot_of]
        .set(jnp.arange(assign_count, dtype=jnp.int32))
    )
    return (slot_of, source)


def run_groups(bundles, hidden_units):
    parties = lax.axis_size("dp")
    row_totals = [bundle[0].shape[0] * bundle[0].shape[1] for bundle in bundles]
    gate_part = jnp.concatenate(
        [
            jnp.einsum(
                "grd,gdf->grf", bundle[0], bundle[2], preferred_element_type=jnp.float32
            ).reshape(-1, hidden_units)
            for bundle in bundles
        ],
        axis=0,
    )
    up_part = jnp.concatenate(
        [
            jnp.einsum(
                "grd,gdf->grf", bundle[0], bundle[3], preferred_element_type=jnp.float32
            ).reshape(-1, hidden_units)
            for bundle in bundles
        ],
        axis=0,
    )
    total_rows = gate_part.shape[0]
    share_rows = total_rows // parties
    share_start = lax.axis_index("dp") * share_rows
    gate_pre, up_pre = (
        lax.psum(gate_part.astype(jnp.bfloat16), "dp").astype(jnp.float32),
        lax.psum(up_part.astype(jnp.bfloat16), "dp").astype(jnp.float32),
    )
    hidden = (jax.nn.silu(gate_pre) * up_pre).astype(jnp.bfloat16)
    gate_share = lax.dynamic_slice_in_dim(gate_pre, share_start, share_rows, 0)
    up_share = lax.dynamic_slice_in_dim(up_pre, share_start, share_rows, 0)
    hidden_part = jnp.concatenate(
        [
            jnp.einsum(
                "grd,gfd->grf", bundle[1], bundle[4], preferred_element_type=jnp.float32
            ).reshape(-1, hidden_units)
            for bundle in bundles
        ],
        axis=0,
    )
    hidden_grad = lax.psum_scatter(
        hidden_part.astype(jnp.bfloat16), "dp", scatter_dimension=0, tiled=True
    ).astype(jnp.float32)
    sigmoid_g = jax.nn.sigmoid(gate_share)
    gate_grad = (
        hidden_grad * up_share * sigmoid_g * (1.0 + gate_share * (1.0 - sigmoid_g))
    ).astype(jnp.bfloat16)
    up_grad = (hidden_grad * gate_share * sigmoid_g).astype(jnp.bfloat16)
    gate_rows, up_rows = (
        lax.all_gather(gate_grad, "dp", axis=0, tiled=True),
        lax.all_gather(up_grad, "dp", axis=0, tiled=True),
    )
    outputs = []
    offset = 0
    for bundle, row_total in zip(bundles, row_totals):
        piece_shape = (bundle[0].shape[0], bundle[0].shape[1], hidden_units)
        hidden_piece = hidden.reshape(piece_shape)
        gate_piece = gate_rows.reshape(piece_shape)
        up_piece = up_rows.reshape(piece_shape)
        offset = offset + row_total
        expert_out = jnp.einsum(
            "grf,gfd->grd", hidden_piece, bundle[4], preferred_element_type=jnp.float32
        ).astype(jnp.bfloat16)
        slot_grad = (
            jnp.einsum("grf,gdf->grd", gate_piece, bundle[2], preferred_element_type=jnp.float32)
            + jnp.einsum("grf,gdf->grd", up_piece, bundle[3], preferred_element_type=jnp.float32)
        ).astype(jnp.bfloat16)
        dw_gate = jnp.einsum(
            "grd,grf->gdf", bundle[0], gate_piece, preferred_element_type=jnp.float32
        )
        dw_up = jnp.einsum("grd,grf->gdf", bundle[0], up_piece, preferred_element_type=jnp.float32)
        dw_down = jnp.einsum(
            "grf,grd->gfd", hidden_piece, bundle[1], preferred_element_type=jnp.float32
        )
        outputs.append((expert_out, slot_grad, dw_gate, dw_up, dw_down))
    return outputs


def on_device(tokens, expert_ids, gate_prob, w_gate, w_up, w_down, grad_out):
    tok_rows, fanout = expert_ids.shape
    per_device, slice_width, hidden_units = w_gate.shape
    columns = lax.axis_size("expert")
    capacity = 2 * tok_rows * fanout // (per_device * columns)
    slot_count = per_device * columns * capacity
    assign_count = tok_rows * fanout
    slot_of, source = slot_tables(expert_ids, columns, per_device, capacity)
    filled = source < assign_count
    safe_src = jnp.minimum(source, assign_count - 1)
    tok_index = safe_src // fanout
    gate_flat = gate_prob.reshape(-1)
    token_buffer = jnp.where(filled[:, None], tokens[tok_index], jnp.zeros((), jnp.bfloat16))
    gate_slots = jnp.where(filled, gate_flat[safe_src], jnp.zeros((), jnp.float32))
    grad_buffer = (gate_slots[:, None] * grad_out[tok_index].astype(jnp.float32)).astype(
        jnp.bfloat16
    )
    layout = (per_device, columns, capacity, slice_width)
    sent_tokens, sent_grads = (
        lax.all_to_all(
            token_buffer.reshape(layout), "expert", split_axis=1, concat_axis=1, tiled=True
        ),
        lax.all_to_all(
            grad_buffer.reshape(layout), "expert", split_axis=1, concat_axis=1, tiled=True
        ),
    )
    bundles = [
        (
            sent_tokens.reshape(per_device, columns * capacity, slice_width),
            sent_grads.reshape(per_device, columns * capacity, slice_width),
            w_gate,
            w_up,
            w_down,
        )
    ]
    results = run_groups(bundles, hidden_units)
    expert_out = results[0][0].reshape(layout)
    slot_grad = results[0][1].reshape(layout)
    total_gate = results[0][2]
    total_up = results[0][3]
    total_down = results[0][4]
    grad_w_gate = total_gate.astype(jnp.bfloat16)
    grad_w_up = total_up.astype(jnp.bfloat16)
    grad_w_down = total_down.astype(jnp.bfloat16)
    back_out, back_grad = (
        lax.all_to_all(expert_out, "expert", split_axis=1, concat_axis=1, tiled=True),
        lax.all_to_all(slot_grad, "expert", split_axis=1, concat_axis=1, tiled=True),
    )
    out_rows = (
        back_out.reshape(slot_count, slice_width)[slot_of]
        .reshape(tok_rows, fanout, slice_width)
        .astype(jnp.float32)
    )
    grad_rows = (
        back_grad.reshape(slot_count, slice_width)[slot_of]
        .reshape(tok_rows, fanout, slice_width)
        .astype(jnp.float32)
    )
    mixed = jnp.sum(gate_prob[:, :, None] * out_rows, axis=1).astype(jnp.bfloat16)
    grad_tokens = jnp.sum(grad_rows, axis=1).astype(jnp.bfloat16)
    partial_dots = jnp.sum(out_rows * grad_out.astype(jnp.float32)[:, None, :], axis=2)
    grad_gate = lax.psum(partial_dots, "dp")
    return (mixed, grad_tokens, grad_gate, grad_w_gate, grad_w_up, grad_w_down)


def solution(mesh):
    return jax.shard_map(
        on_device,
        mesh=mesh,
        in_specs=(
            P("expert", "dp"),
            P("expert", None),
            P("expert", None),
            P("expert", "dp", None),
            P("expert", "dp", None),
            P("expert", None, "dp"),
            P("expert", "dp"),
        ),
        out_specs=(
            P("expert", "dp"),
            P("expert", "dp"),
            P("expert", None),
            P("expert", "dp", None),
            P("expert", "dp", None),
            P("expert", None, "dp"),
        ),
        check_vma=False,
    )
```

profile of v0, /device:TPU:0, one launch (start us, length us, event | category | flops | bytes accessed | tf_op | source)
XLA Modules:
  0.0 420.2 jit_solution(9456463148438041457)
XLA Ops:
  7.2 0.9 copy.49
  8.4 0.8 copy.48
  9.3 4.5 %reduce-window.6 = s32[16,8,128]{2,1,0:T(8,128)S(1)} reduce-window(s32[16,8,128]{2,1,0:T(8,128)S(1)} %fusion.11, s32[]{:T(128)} %constant.59.clone.1), window={size=1x1x128 pad=0_0x0_0x127_0}, to_apply=%region_0.0 | reduce-window | flops 2080768 | bytes 131076 | tf_op jit(solution)/shard_map/reduce-window
  13.9 0.1 copy.52
  14.3 4.3 %scatter_custom_fusion = s32[2048]{0:T(1024)S(1)} fusion(s32[1024]{0:T(1024)S(1)} %bitcast.87, s32[1024]{0:T(1024)S(1)} %iota.11, s32[]{:T(128)} %constant.58.clone.1), kind=kCustom, calls=%fused_computation.60 | custom fusion | bytes 8196 | tf_op jit(solution)/shard_map/scatter | solution.py:21
  18.7 8.6 %gather_fusion.2 = f32[2048]{0:T(1024)S(1)} fusion(f32[1024]{0:T(1024)S(1)} %reshape.230, s32[2048]{0:T(1024)S(1)} %get-tuple-element.26), kind=kCustom, calls=%fused_computation.2 | custom fusion | bytes 24576 | tf_op jit(solution)/shard_map/gather | solution.py:117
  27.3 9.2 %gather_fusion = bf16[2048,512]{1,0:T(8,128)(2,1)} fusion(bf16[128,512]{1,0:T(8,128)(2,1)S(1)} %copy-done.2, s32[2048]{0:T(1024)S(1)} %get-tuple-element.27), kind=kCustom, calls=%fused_computation | custom fusion | bytes 4202496 | tf_op jit(solution)/shard_map/gather | solution.py:116
  36.5 2.7 copy_select_fusion
  39.3 6.4 %all-to-all-start = ((bf16[4,4,128,512]{3,2,0,1:T(8,128)(2,1)}), bf16[4,4,128,512]{3,2,0,1:T(8,128)(2,1)}, u32[]{:S(2)}, u32[]{:S(2)}) async-start(bf16[4,4,128,512]{3,2,0,1:T(8,128)(2,1)} %copy_select_fusion), calls=%async_computation | async-start | bytes 4194304 | tf_op jit(solution)/shard_map/all_to_all | solution.py:123
  45.7 9.2 %gather_fusion.3 = bf16[2048,512]{1,0:T(8,128)(2,1)} fusion(bf16[128,512]{1,0:T(8,128)(2,1)S(1)} %copy-done.1, s32[2048]{0:T(1024)S(1)} %get-tuple-element.27), kind=kCustom, calls=%fused_computation.3 | custom fusion | bytes 4202496 | tf_op jit(solution)/shard_map/gather | solution.py:118
  54.9 3.4 fusion
  58.3 35.7 %all-to-all-done = bf16[4,4,128,512]{3,2,0,1:T(8,128)(2,1)} async-done(((bf16[4,4,128,512]{3,2,0,1:T(8,128)(2,1)}), bf16[4,4,128,512]{3,2,0,1:T(8,128)(2,1)}, u32[]{:S(2)}, u32[]{:S(2)}) %all-to-all-start) | async-done | bytes 2097184 | tf_op jit(solution)/shard_map/all_to_all | solution.py:123
  94.0 4.4 %all-to-all-start.2 = ((bf16[4,4,128,512]{3,2,0,1:T(8,128)(2,1)}), bf16[4,4,128,512]{3,2,0,1:T(8,128)(2,1)}, u32[]{:S(2)}, u32[]{:S(2)}) async-start(bf16[4,4,128,512]{3,2,0,1:T(8,128)(2,1)} %fusion), calls=%async_computation.2 | async-start | bytes 4194304 | tf_op jit(solution)/shard_map/all_to_all | solution.py:126
  98.6 1.9 copy.56
  100.5 0.6 copy-done.5
  101.1 3.5 convolution_convert_fusion.4
  104.5 3.5 convolution_convert_fusion.5
  108.1 38.2 %all-to-all-done.2 = bf16[4,4,128,512]{3,2,0,1:T(8,128)(2,1)} async-done(((bf16[4,4,128,512]{3,2,0,1:T(8,128)(2,1)}), bf16[4,4,128,512]{3,2,0,1:T(8,128)(2,1)}, u32[]{:S(2)}, u32[]{:S(2)}) %all-to-all-start.2) | async-done | bytes 2097184 | tf_op jit(solution)/shard_map/all_to_all | solution.py:126
  146.3 1.8 copy.62
  148.1 3.5 convolution_convert_fusion.3
  151.7 62.3 %all-reduce.3.cloned.1.call-done = (bf16[2048,768]{1,0:T(8,128)(2,1)}, bf16[2048,768]{1,0:T(8,128)(2,1)}) async-done(((bf16[2048,768]{1,0:T(8,128)(2,1)}, bf16[2048,768]{1,0:T(8,128)(2,1)}), (bf16[2048,768]{1,0:T(8,128)(2,1)}, bf16[2048,768]{1,0:T(8,128)(2,1)})) %all-reduce.3.cloned.1.call-update) | async-done | bytes 6291472 | tf_op jit(solution)/shard_map/psum | solution.py:52
  213.9 5.2 %convert_element_type.91 = f32[2048,768]{1,0:T(8,128)} convert(bf16[2048,768]{1,0:T(8,128)(2,1)} %get-tuple-element.21) | non-fusion elementwise | flops 1572864 | bytes 9437184 | tf_op jit(solution)/shard_map/convert_element_type | solution.py:51
  219.1 3.1 convert_element_type.94
  222.3 42.4 %reduce-scatter.2.cloned.1.call-done = bf16[256,768]{1,0:T(8,128)(2,1)} async-done(((bf16[2048,768]{1,0:T(8,128)(2,1)}), bf16[256,768]{1,0:T(8,128)(2,1)}) %reduce-scatter.2.cloned.1.call-update) | async-done | bytes 393232 | tf_op jit(solution)/shard_map/reduce_scatter | solution.py:66
  264.7 2.7 fusion.7
  267.4 0.2 all-gather.5.cloned.1.call-start
  267.6 0.3 all-gather.5.cloned.1.call-update
  268.0 3.8 multiply_convert_fusion
  271.8 1.8 convolution_convert_fusion.6
  273.7 1.5 copy.57
  275.2 4.6 %all-to-all-start.1 = ((bf16[4,4,128,512]{3,2,0,1:T(8,128)(2,1)}), bf16[4,4,128,512]{3,2,0,1:T(8,128)(2,1)}, u32[]{:S(2)}, u32[]{:S(2)}) async-start(bf16[4,4,128,512]{3,2,0,1:T(8,128)(2,1)} %copy.57), calls=%async_computation.1 | async-start | bytes 4194304 | tf_op jit(solution)/shard_map/all_to_all | solution.py:149
  279.8 20.1 %all-gather.3.cloned.1.call-done = bf16[2048,768]{1,0:T(8,128)(2,1)} async-done(((bf16[256,768]{1,0:T(8,128)(2,1)}), bf16[2048,768]{1,0:T(8,128)(2,1)}) %all-gather.3.cloned.1.call-update) | async-done | bytes 3145744 | tf_op jit(solution)/shard_map/all_gather | solution.py:75
  299.9 6.6 %fusion.20 = f32[4,512,512]{2,1,0:T(8,128)} fusion(bf16[4,512,768]{2,1,0:T(8,128)(2,1)} %bitcast.70, bf16[4,512,768]{2,1,0:T(8,128)(2,1)} %param.10), kind=kOutput, calls=%fused_computation.63 | convolution fusion | flops 1610612736 | bytes 10485760 | tf_op jit(solution)/shard_map/grf,gdf->grd/dot_general | solution.py:90
  306.5 28.0 %all-gather.5.cloned.1.call-done = bf16[2048,768]{1,0:T(8,128)(2,1)} async-done(((bf16[256,768]{1,0:T(8,128)(2,1)}), bf16[2048,768]{1,0:T(8,128)(2,1)}) %all-gather.5.cloned.1.call-update) | async-done | bytes 3145744 | tf_op jit(solution)/shard_map/all_gather | solution.py:76
  334.5 5.9 %add_convert_fusion = bf16[4,512,512]{2,1,0:T(8,128)(2,1)S(1)} fusion(f32[4,512,512]{2,1,0:T(8,128)} %fusion.20, bf16[4,512,768]{2,1,0:T(8,128)(2,1)} %bitcast.72, bf16[4,512,768]{2,1,0:T(8,128)(2,1)} %param.11), kind=kOutput, calls=%fused_computation.9 | convolution fusion | flops 1612709888 | bytes 12582912 | tf_op jit(solution)/shard_map/grf,gdf->grd/dot_general | solution.py:91
  340.4 1.5 copy.63
  341.9 4.6 %all-to-all-start.3 = ((bf16[4,4,128,512]{3,2,0,1:T(8,128)(2,1)}), bf16[4,4,128,512]{3,2,0,1:T(8,128)(2,1)}, u32[]{:S(2)}, u32[]{:S(2)}) async-start(bf16[4,4,128,512]{3,2,0,1:T(8,128)(2,1)} %copy.63), calls=%async_computation.4 | async-start | bytes 4194304 | tf_op jit(solution)/shard_map/all_to_all | solution.py:150
  346.5 6.0 %convolution_convert_fusion = bf16[4,768,512]{2,1,0:T(8,128)(2,1)} fusion(bf16[4,512,768]{2,1,0:T(8,128)(2,1)} %bitcast.75, bf16[4,512,512]{2,1,0:T(8,128)(2,1)} %bitcast.81), kind=kOutput, calls=%fused_computation.12 | convolution fusion | flops 1612185600 | bytes 8388608 | tf_op jit(solution)/shard_map/grf,grd->gfd/dot_general | solution.py:97
  352.6 3.1 copy.58
  355.7 7.0 %gather_fusion.1 = bf16[1024,512]{1,0:T(8,128)(2,1)} fusion(bf16[2048,512]{1,0:T(8,128)(2,1)} %bitcast.63, s32[1024]{0:T(1024)S(1)} %broadcast_clamp_fusion), kind=kCustom, calls=%fused_computation.1 | custom fusion | bytes 2101248 | tf_op jit(solution)/shard_map/gather | solution.py:153
  362.7 2.9 fusion.2
  365.6 25.0 %psum.23 = f32[128,8]{1,0:T(8,128)S(1)} all-reduce(f32[128,8]{1,0:T(8,128)S(1)} %get-tuple-element.18), channel_id=1, replica_groups=mesh['dp'=8,'expert'=4] {'dp'}, use_global_device_ids=true, to_apply=%region_10.11 | all-reduce | flops 1024 | bytes 8192 | tf_op jit(solution)/shard_map/psum | solution.py:165
  390.6 0.7 copy.68
  391.3 6.2 %convolution_convert_fusion.2 = bf16[4,512,768]{2,1,0:T(8,128)(2,1)} fusion(bf16[4,512,512]{2,1,0:T(8,128)(2,1)} %bitcast.78, bf16[4,512,768]{2,1,0:T(8,128)(2,1)} %bitcast.71), kind=kOutput, calls=%fused_computation.14 | convolution fusion | flops 1612185600 | bytes 8388608 | tf_op jit(solution)/shard_map/grd,grf->gdf/dot_general | solution.py:93
  397.4 3.6 convolution_convert_fusion.1
  401.0 3.1 copy.64
  404.1 6.9 %gather_fusion.4 = bf16[1024,512]{1,0:T(8,128)(2,1)} fusion(bf16[2048,512]{1,0:T(8,128)(2,1)} %bitcast.62, s32[1024]{0:T(1024)S(1)} %broadcast_clamp_fusion), kind=kCustom, calls=%fused_computation.4 | custom fusion | bytes 2101248 | tf_op jit(solution)/shard_map/gather | solution.py:158
  411.1 2.6 bitcast_reduce_fusion
  (52 shorter events, 1.0 us)
Async XLA Ops:
  7.2 140.9 %copy-start = (bf16[4,768,512]{2,1,0:T(8,128)(2,1)S(1)}, bf16[4,768,512]{2,1,0:T(8,128)(2,1)}, u32[]{:S(2)}) copy-start(bf16[4,768,512]{2,1,0:T(8,128)(2,1)} %param.12) | copy-start | bytes 9437188
  9.2 18.1 %copy-start.11 = (f32[128,8]{1,0:T(8,128)}, f32[128,8]{1,0:T(8,128)S(1)}, u32[]{:S(2)}) copy-start(f32[128,8]{1,0:T(8,128)S(1)} %copy.48) | copy-start | bytes 12292
  18.7 8.6 %copy-start.2 = (bf16[128,512]{1,0:T(8,128)(2,1)S(1)}, bf16[128,512]{1,0:T(8,128)(2,1)}, u32[]{:S(2)}) copy-start(bf16[128,512]{1,0:T(8,128)(2,1)} %param.7) | copy-start | bytes 393220
  39.3 6.5 %copy-start.1 = (bf16[128,512]{1,0:T(8,128)(2,1)S(1)}, bf16[128,512]{1,0:T(8,128)(2,1)}, u32[]{:S(2)}) copy-start(bf16[128,512]{1,0:T(8,128)(2,1)} %param.13) | copy-start | bytes 393220
  39.3 54.8 %all-to-all-start = ((bf16[4,4,128,512]{3,2,0,1:T(8,128)(2,1)}), bf16[4,4,128,512]{3,2,0,1:T(8,128)(2,1)}, u32[]{:S(2)}, u32[]{:S(2)}) async-start(bf16[4,4,128,512]{3,2,0,1:T(8,128)(2,1)} %copy_select_fusion), calls=%async_computation | async-start | bytes 4194304 | tf_op jit(solution)/shard_map/all_to_all | solution.py:123
  94.0 52.2 %all-to-all-start.2 = ((bf16[4,4,128,512]{3,2,0,1:T(8,128)(2,1)}), bf16[4,4,128,512]{3,2,0,1:T(8,128)(2,1)}, u32[]{:S(2)}, u32[]{:S(2)}) async-start(bf16[4,4,128,512]{3,2,0,1:T(8,128)(2,1)} %fusion), calls=%async_computation.2 | async-start | bytes 4194304 | tf_op jit(solution)/shard_map/all_to_all | solution.py:126
  98.5 115.5 %all-reduce.3.cloned.1.call-start = ((), (), s32[]{:S(2)}) async-start(), calls=%async_computation.8 | async-start | bytes 12582912 | tf_op jit(solution)/shard_map/psum | solution.py:52
  98.5 2.5 copy-start.5
  100.5 4.1 copy-start.8
  101.1 3.5 copy-start.4
  108.0 156.6 %reduce-scatter.2.cloned.1.call-start = ((), (), s32[]{:S(2)}) async-start(), calls=%async_computation.5 | async-start | bytes 3538944 | tf_op jit(solution)/shard_map/reduce_scatter | solution.py:66
  148.1 3.5 copy-start.10
  151.6 148.3 %all-gather.3.cloned.1.call-start = ((), (), s32[]{:S(2)}) async-start(), calls=%async_computation.6 | async-start | bytes 3538944 | tf_op jit(solution)/shard_map/all_gather | solution.py:75
  213.9 5.2 %copy-start.3 = (bf16[2048,768]{1,0:T(8,128)(2,1)S(1)}, bf16[2048,768]{1,0:T(8,128)(2,1)}, u32[]{:S(2)}) copy-start(bf16[2048,768]{1,0:T(8,128)(2,1)} %get-tuple-element.20) | copy-start | bytes 9437188
  267.4 67.1 %all-gather.5.cloned.1.call-start = ((), (), s32[]{:S(2)}) async-start(), calls=%async_computation.7 | async-start | bytes 3538944 | tf_op jit(solution)/shard_map/all_gather | solution.py:76
  271.8 1.8 copy-start.7
  275.2 66.7 %all-to-all-start.1 = ((bf16[4,4,128,512]{3,2,0,1:T(8,128)(2,1)}), bf16[4,4,128,512]{3,2,0,1:T(8,128)(2,1)}, u32[]{:S(2)}, u32[]{:S(2)}) async-start(bf16[4,4,128,512]{3,2,0,1:T(8,128)(2,1)} %copy.57), calls=%async_computation.1 | async-start | bytes 4194304 | tf_op jit(solution)/shard_map/all_to_all | solution.py:149
  341.9 59.1 %all-to-all-start.3 = ((bf16[4,4,128,512]{3,2,0,1:T(8,128)(2,1)}), bf16[4,4,128,512]{3,2,0,1:T(8,128)(2,1)}, u32[]{:S(2)}, u32[]{:S(2)}) async-start(bf16[4,4,128,512]{3,2,0,1:T(8,128)(2,1)} %copy.63), calls=%async_computation.4 | async-start | bytes 4194304 | tf_op jit(solution)/shard_map/all_to_all | solution.py:150
  355.7 7.0 %copy-start.12 = (f32[128,8]{1,0:T(8,128)S(1)}, f32[128,8]{1,0:T(8,128)}, u32[]{:S(2)}) copy-start(f32[128,8]{1,0:T(8,128)} %copy-done.11) | copy-start | bytes 12292
  391.2 6.2 %copy-start.6 = (bf16[2048,768]{1,0:T(8,128)(2,1)S(1)}, bf16[2048,768]{1,0:T(8,128)(2,1)}, u32[]{:S(2)}) copy-start(bf16[2048,768]{1,0:T(8,128)(2,1)} %all-gather.5.cloned.1.call-done) | copy-start | bytes 9437188
  391.2 6.2 %copy-start.9 = (bf16[4,4,128,512]{3,2,1,0:T(8,128)(2,1)S(1)}, bf16[4,4,128,512]{3,2,1,0:T(8,128)(2,1)}, u32[]{:S(2)}) copy-start(bf16[4,4,128,512]{3,2,1,0:T(8,128)(2,1)} %copy-done.8) | copy-start | bytes 6291460
Sparse Core Ops, SparseCore 0:
  108.2 105.7 all-reduce.2
  218.3 46.3 reduce-scatter.1
  267.5 32.2 all-gather.2
  302.2 32.3 all-gather.4
where the time goes:
time: 421 us; the launch traced here: 420 us
  waiting for transfers between devices  227 us (54%)
  local copies, waits for them, and re-layouts  61.8 us (15%)
  matrix products  40.5 us (10%)
  other arithmetic  31.3 us (7%)
  blocking collectives  25 us (6%)
  starting transfers between devices  20.4 us (5%)
  between operations  14 us (3%)
    psum x1, waiting for transfers between devices, run_groups(): lax.psum(up_part.astype(jnp.bfloat16), 'dp').astype(jnp.float32)  62.3 us
    reduce_scatter x1, waiting for transfers between devices, run_groups(): lax.psum_scatter(hidden_part.astype(jnp.bfloat16), 'dp', scatter_dimensio...  42.4 us
    all_to_all x1, waiting for transfers between devices, on_device(): lax.all_to_all(grad_buffer.reshape(layout), 'expert', split_axis=1, conca...  38.2 us
    all_to_all x1, waiting for transfers between devices, on_device(): lax.all_to_all(token_buffer.reshape(layout), 'expert', split_axis=1, conc...  35.7 us
    all_gather x1, waiting for transfers between devices, run_groups(): lax.all_gather(up_grad, 'dp', axis=0, tiled=True)  28 us
    psum x1, blocking collectives, on_device(): grad_gate = lax.psum(partial_dots, 'dp')  25 us
    all_gather x1, waiting for transfers between devices, run_groups(): lax.all_gather(gate_grad, 'dp', axis=0, tiled=True)  20.1 us
    gather x1, local copies, waits for them, and re-layouts, on_device(): tokens[tok_index]  9.21 us
  transfers between devices with their start and end apart: 8, of which 6 were waited for; matrix products, arithmetic and copies ran while one was open for 20% of the time, Pallas kernels for 0%

commit v1 on v0

v1 whole, which is shorter than its diff:
```python
import jax
import jax.numpy as jnp
from jax import lax
from jax.sharding import PartitionSpec as P


def split_bf16(value):
    high = value.astype(jnp.bfloat16)
    rest = value - high.astype(jnp.float32)
    mid = rest.astype(jnp.bfloat16)
    low = (rest - mid.astype(jnp.float32)).astype(jnp.bfloat16)
    return high, mid, low


def exchange(x_rows, g_rows, probs, w_gate, w_up, w_down):
    per_device, rows, _ = probs.shape
    hidden_units = w_gate.shape[2]
    experts = range(per_device)
    scaled = (probs * g_rows.astype(jnp.float32)).astype(jnp.bfloat16)

    def dot(spec, a, b):
        return jnp.einsum(spec, a, b, preferred_element_type=jnp.float32).astype(jnp.bfloat16)

    x_all = jnp.broadcast_to(x_rows, (per_device,) + x_rows.shape[1:])
    part = jnp.concatenate(
        [
            dot("grd,gdf->grf", x_all, w_gate),
            dot("grd,gdf->grf", x_all, w_up),
            dot("grd,gfd->grf", scaled, w_down),
        ],
        axis=2,
    ).reshape(per_device * rows, 3 * hidden_units)
    share = lax.psum_scatter(part, "dp", scatter_dimension=0, tiled=True).astype(jnp.float32)
    gate, up, hgrad = jnp.split(share, 3, axis=1)
    sig = jax.nn.sigmoid(gate)
    act = jnp.concatenate(
        [gate * sig * up, hgrad * up * sig * (1.0 + gate * (1.0 - sig)), hgrad * gate * sig],
        axis=1,
    ).astype(jnp.bfloat16)
    full = lax.all_gather(act, "dp", axis=0, tiled=True).reshape(per_device, rows, 3 * hidden_units)
    return scaled, full


def on_device(tokens, expert_ids, gate_prob, w_gate, w_up, w_down, grad_out):
    tok_rows, fanout = expert_ids.shape
    per_device, width, hidden_units = w_gate.shape
    columns = lax.axis_size("expert")
    me = lax.axis_index("expert")
    capacity = 2 * tok_rows * fanout // (per_device * columns)
    dense = capacity >= tok_rows
    experts_all = per_device * columns
    picked = expert_ids[:, :, None] == jnp.arange(experts_all, dtype=jnp.int32)
    prob_of = jnp.sum(jnp.where(picked, gate_prob[:, :, None], 0.0), axis=1)
    pad = -3 * experts_all % 128
    packed = jnp.concatenate(
        [tokens, grad_out, *split_bf16(prob_of), jnp.zeros((tok_rows, pad), jnp.bfloat16)], axis=1
    )
    gathered = lax.all_gather(packed, "expert", axis=0, tiled=True)
    count = gathered.shape[0]
    x_all = gathered[:, :width]
    g_all = gathered[:, width : 2 * width]
    pieces = gathered[:, 2 * width : 2 * width + 3 * experts_all].astype(jnp.float32)
    pieces = pieces.reshape(count, 3, experts_all)
    prob_all = pieces[:, 0] + pieces[:, 1] + pieces[:, 2]
    prob_here = lax.dynamic_slice_in_dim(prob_all, me * per_device, per_device, 1).T
    if dense:
        x_rows, g_rows, probs = x_all[None], g_all[None], prob_here[:, :, None]
    else:
        blocks = prob_here.reshape(per_device, columns, tok_rows)
        chosen = (blocks > 0).astype(jnp.int32)
        rank = jnp.cumsum(chosen, axis=2) - 1
        slots = jnp.arange(capacity, dtype=jnp.int32)[:, None]
        hit = (rank[:, :, None, :] == slots) & (chosen[:, :, None, :] > 0)
        local = jnp.sum(jnp.where(hit, jnp.arange(tok_rows, dtype=jnp.int32), 0), axis=3)
        row_of = local + jnp.arange(columns, dtype=jnp.int32)[:, None] * tok_rows
        row_of = row_of.reshape(per_device, columns * capacity)
        x_rows, g_rows = x_all[row_of], g_all[row_of]
        probs = jnp.sum(jnp.where(hit, blocks[:, :, None, :], 0.0), axis=3)
        probs = probs.reshape(per_device, columns * capacity, 1)
    scaled, full = exchange(x_rows, g_rows, probs, w_gate, w_up, w_down)
    hidden = full[:, :, :hidden_units]
    gate_grad = full[:, :, hidden_units : 2 * hidden_units]
    up_grad = full[:, :, 2 * hidden_units :]

    def dot(spec, a, b):
        return jnp.einsum(spec, a, b, preferred_element_type=jnp.float32)

    out = dot("grf,gfd->grd", hidden, w_down).astype(jnp.bfloat16).astype(jnp.float32)
    back = (dot("grf,gdf->grd", gate_grad, w_gate) + dot("grf,gdf->grd", up_grad, w_up)).astype(
        jnp.bfloat16
    )
    dots = jnp.sum(out * g_rows.astype(jnp.float32), axis=2)
    if dense:
        mixed_part = jnp.sum(probs * out, axis=0)
        grad_part = jnp.sum(back.astype(jnp.float32), axis=0)
        dots_of = jnp.where(prob_here > 0, dots, 0.0)
    else:
        flat = row_of.reshape(-1)
        start = jnp.zeros((count, width), jnp.float32)
        mixed_part = start.at[flat].add((probs * out).reshape(-1, width))
        real = jnp.where(probs > 0, back.astype(jnp.float32), 0.0)
        grad_part = start.at[flat].add(real.reshape(-1, width))
        expert_at = jnp.arange(per_device, dtype=jnp.int32)[:, None]
        dots_of = jnp.zeros((per_device, count), jnp.float32).at[expert_at, row_of].add(
            jnp.where(probs[:, :, 0] > 0, dots, 0.0)
        )
    parts = jnp.concatenate([mixed_part, grad_part], axis=1).astype(jnp.bfloat16)
    summed = lax.psum_scatter(parts, "expert", scatter_dimension=0, tiled=True)
    mixed, grad_tokens = summed[:, :width], summed[:, width:]
    wide = jnp.zeros((count, experts_all), jnp.float32)
    wide = lax.dynamic_update_slice_in_dim(wide, dots_of.T, me * per_device, 1)
    wide = lax.psum_scatter(wide, "expert", scatter_dimension=0, tiled=True)
    grad_gate = lax.psum(
        jnp.sum(jnp.where(picked, wide[:, None, :], 0.0), axis=2), "dp"
    )
    x_b = jnp.broadcast_to(x_rows, (per_device,) + x_rows.shape[1:])
    grad_w_gate = dot("grd,grf->gdf", x_b, gate_grad).astype(jnp.bfloat16)
    grad_w_up = dot("grd,grf->gdf", x_b, up_grad).astype(jnp.bfloat16)
    grad_w_down = dot("grf,grd->gfd", hidden, scaled).astype(jnp.bfloat16)
    return (mixed, grad_tokens, grad_gate, grad_w_gate, grad_w_up, grad_w_down)


def solution(mesh):
    return jax.shard_map(
        on_device,
        mesh=mesh,
        in_specs=(
            P("expert", "dp"),
            P("expert", None),
            P("expert", None),
            P("expert", "dp", None),
            P("expert", "dp", None),
            P("expert", None, "dp"),
            P("expert", "dp"),
        ),
        out_specs=(
            P("expert", "dp"),
            P("expert", "dp"),
            P("expert", None),
            P("expert", "dp", None),
            P("expert", "dp", None),
            P("expert", None, "dp"),
        ),
        check_vma=False,
    )
```

time: 421 us -> 267 us (0.63)
  waiting for transfers between devices: 227 us -> 170 us
  local copies, waits for them, and re-layouts: 61.8 us -> 14.1 us
  starting transfers between devices: 20.4 us -> 0.39 us
  other arithmetic: 31.3 us -> 12.5 us
  blocking collectives: 25 us -> 14.3 us
    all_to_all x4 -> x0, waiting for transfers between devices: 73.9 us -> none  [the longest x1 38.2 us: on_device(): lax.all_to_all(grad_buffer.reshape(layout), 'expert', split_axis=1, conca...]
    psum x1 -> x0, waiting for transfers between devices: 62.3 us -> none  [run_groups(): lax.psum(up_part.astype(jnp.bfloat16), 'dp').astype(jnp.float32)]
    all_gather x2, waiting for transfers between devices: 48.1 us -> 93.5 us  [the longest x1 58.9 us: exchange(): lax.all_gather(act, 'dp', axis=0, tiled=True)]
    gather x5 -> x0, local copies, waits for them, and re-layouts: 40.9 us -> none  [the longest x1 9.21 us: on_device(): tokens[tok_index]]
    reduce_scatter x1 -> x2, waiting for transfers between devices: 42.4 us -> 74.9 us  [the longest x1 74.9 us: exchange(): lax.psum_scatter(part, 'dp', scatter_dimension=0, tiled=True)]
    all_to_all x4 -> x0, starting transfers between devices: 20.1 us -> none  [the longest x1 6.45 us: on_device(): lax.all_to_all(token_buffer.reshape(layout), 'expert', split_axis=1, conc...]
    convert_element_type x7 -> x1, other arithmetic: 18.3 us -> 1.42 us  [exchange(): lax.psum_scatter(part, 'dp', scatter_dimension=0, tiled=True)]
    psum x1, blocking collectives: 25 us -> 14.3 us  [on_device(): lax.psum(jnp.sum(jnp.where(picked, wide[:, None, :], 0.0), axis=2), 'dp')]
  transfers between devices with their start and end apart: 8 -> 5, of which waited for: 6 -> 4; matrix products, arithmetic and copies ran while one was open for 20% -> 12% of each run, Pallas kernels for 0% -> 0%
where the time goes in v1:
time: 267 us; the launch traced here: 266 us
  waiting for transfers between devices  170 us (64%)
  matrix products  41.4 us (16%)
  blocking collectives  14.3 us (5%)
  local copies, waits for them, and re-layouts  14.1 us (5%)
  between operations  13.9 us (5%)
  other arithmetic  12.5 us (5%)
    reduce_scatter x1, waiting for transfers between devices, exchange(): lax.psum_scatter(part, 'dp', scatter_dimension=0, tiled=True)  74.9 us
    all_gather x1, waiting for transfers between devices, exchange(): lax.all_gather(act, 'dp', axis=0, tiled=True)  58.9 us
    dot_general x6, matrix products, dot(): return jnp.einsum(spec, a, b, preferred_element_type=jnp.float32)  35.6 us
    all_gather x1, waiting for transfers between devices, on_device(): gathered = lax.all_gather(packed, 'expert', axis=0, tiled=True)  34.6 us
    psum x1, blocking collectives, on_device(): lax.psum(jnp.sum(jnp.where(picked, wide[:, None, :], 0.0), axis=2), 'dp')  14.3 us
    unnamed x25, local copies, waits for them, and re-layouts  9.5 us
    dot_general x3, matrix products, dot(): jnp.einsum(spec, a, b, preferred_element_type=jnp.float32)  5.87 us
  transfers between devices with their start and end apart: 5, of which 4 were waited for; matrix products, arithmetic and copies ran while one was open for 12% of the time, Pallas kernels for 0%

profile of v1, /device:TPU:0, one launch (start us, length us, event | category | flops | bytes accessed | tf_op | source)
XLA Modules:
  0.0 266.1 jit_solution(7316161283469545302)
XLA Ops:
  7.2 0.0 copy-start
  7.2 0.0 all-gather.3.cloned.1.call-start
  7.2 1.8 copy.63
  9.0 0.9 constant_dynamic-update-slice_fusion.5
  10.0 1.7 copy.64
  11.6 0.7 select_reduce_fusion.1
  12.3 0.9 constant_dynamic-update-slice_fusion.4
  13.3 0.0 copy-start.3
  13.3 0.7 copy-done.3
  14.0 0.0 all-gather.3.cloned.1.call-update
  14.1 0.0 reduce-scatter.6.cloned.1.call-start
  14.1 34.6 %all-gather.3.cloned.1.call-done = bf16[512,1152]{0,1:T(8,128)(2,1)} async-done(((bf16[128,1152]{0,1:T(8,128)(2,1)}), bf16[512,1152]{0,1:T(8,128)(2,1)}) %all-gather.3.cloned.1.call-update) | async-done | bytes 1179664 | tf_op jit(solution)/shard_map/all_gather | solution.py:58
  48.7 0.8 slice.44
  49.5 1.4 fusion.42
  50.9 0.0 copy-start.4
  50.9 0.0 copy-start.9
  50.9 1.8 convolution_convert_fusion
  52.8 0.6 copy-done.9
  53.4 1.9 convolution_convert_fusion.1
  55.3 2.2 fusion.15
  57.4 4.4 %pad_maximum_fusion = bf16[4,512,2304]{2,1,0:T(8,128)(2,1)} fusion(bf16[4,512,768]{2,1,0:T(8,128)(2,1)S(1)} %fusion.15, bf16[4,512,768]{2,1,0:T(8,128)(2,1)S(1)} %convolution_convert_fusion, bf16[4,512,768]{2,1,0:T(8,128)(2,1)S(1)} %convolution_convert_fusion.1), kind=kLoop, calls=%fused_computation | loop fusion | flops 28311552 | bytes 18874368 | tf_op jit(solution)/shard_map/concatenate | solution.py:25
  61.8 0.0 reduce-scatter.6.cloned.1.call-update
  61.8 0.0 all-gather.5.cloned.1.call-start
  61.9 74.9 %reduce-scatter.6.cloned.1.call-done = bf16[256,2304]{1,0:T(8,128)(2,1)} async-done(((bf16[2048,2304]{1,0:T(8,128)(2,1)}), bf16[256,2304]{1,0:T(8,128)(2,1)}) %reduce-scatter.6.cloned.1.call-update) | async-done | bytes 1179664 | tf_op jit(solution)/shard_map/reduce_scatter | solution.py:33
  136.8 1.4 convert_element_type.69
  138.2 0.5 multiply_convert_fusion.9
  138.7 1.1 pad_maximum_fusion.1
  139.8 0.0 all-gather.5.cloned.1.call-update
  139.8 0.0 reduce-scatter.8.cloned.1.call-start
  139.9 58.9 %all-gather.5.cloned.1.call-done = bf16[2048,2304]{1,0:T(8,128)(2,1)} async-done(((bf16[256,2304]{1,0:T(8,128)(2,1)}), bf16[2048,2304]{1,0:T(8,128)(2,1)}) %all-gather.5.cloned.1.call-update) | async-done | bytes 9437200 | tf_op jit(solution)/shard_map/all_gather | solution.py:40
  198.8 6.0 %fusion.1 = (f32[4,512]{1,0:T(4,128)S(1)}, bf16[512,512]{0,1:T(8,128)(2,1)}) fusion(f32[512,512]{0,1:T(8,128)} %copy-done.1, f32[4,512]{1,0:T(4,128)S(1)} %fusion.41, bf16[4,768,512]{2,1,0:T(8,128)(2,1)} %param.12, bf16[4,512,2304]{2,1,0:T(8,128)(2,1)} %bitcast.24), kind=kOutput, calls=%fused_computation.4 | convolution fusion | flops 1616640000 | bytes 7880704 | tf_op jit(solution)/shard_map/grf,gfd->grd/dot_general | solution.py:86
  204.8 5.8 %fusion.6 = f32[4,512,512]{2,1,0:T(8,128)} fusion(bf16[4,512,768]{2,1,0:T(8,128)(2,1)S(1)} %copy-done, bf16[4,512,2304]{2,1,0:T(8,128)(2,1)} %bitcast.25), kind=kOutput, calls=%fused_computation.11 | convolution fusion | flops 1610612736 | bytes 10485760 | tf_op jit(solution)/shard_map/grf,gdf->grd/dot_general | solution.py:86
  210.6 0.0 copy-start.6
  210.6 0.6 copy-done.6
  211.2 0.0 reduce-scatter.8.cloned.1.call-update
  211.2 0.2 reduce-scatter.10.cloned.1.call-start
  211.5 6.9 %fusion.25 = bf16[512,512]{1,0:T(8,128)(2,1)} fusion(f32[4,512,512]{2,1,0:T(8,128)} %fusion.6, bf16[4,512,768]{2,1,0:T(8,128)(2,1)} %param.10, bf16[4,512,2304]{2,1,0:T(8,128)(2,1)} %bitcast.26), kind=kOutput, calls=%fused_computation.26 | convolution fusion | flops 1613496320 | bytes 11010048 | tf_op jit(solution)/shard_map/grf,gdf->grd/dot_general | solution.py:86
  218.4 2.0 copy.69
  220.4 2.2 pad_maximum_fusion.2
  222.6 2.3 copy.80
  224.9 0.0 reduce-scatter.10.cloned.1.call-update
  224.9 5.6 %fusion.19 = bf16[4,512,768]{2,1,0:T(8,128)(2,1)} fusion(bf16[4,512,2304]{2,1,0:T(8,128)(2,1)} %bitcast.27, bf16[512,512]{0,1:T(8,128)(2,1)} %copy-done.4), kind=kOutput, calls=%fused_computation.22 | convolution fusion | flops 1612185600 | bytes 6815744 | tf_op jit(solution)/shard_map/grd,grf->gdf/dot_general | solution.py:86
  230.5 5.4 %fusion.22 = bf16[4,512,768]{2,1,0:T(8,128)(2,1)} fusion(bf16[4,512,2304]{2,1,0:T(8,128)(2,1)} %bitcast.28, bf16[512,512]{0,1:T(8,128)(2,1)S(1)} %copy-done.5), kind=kOutput, calls=%fused_computation.23 | convolution fusion | flops 1612185600 | bytes 6815744 | tf_op jit(solution)/shard_map/grd,grf->gdf/dot_general | solution.py:86
  236.0 5.9 %fusion.16 = bf16[4,768,512]{2,1,0:T(8,128)(2,1)} fusion(bf16[4,512,2304]{2,1,0:T(8,128)(2,1)} %bitcast.29, f32[512,512]{0,1:T(8,128)S(1)} %copy-done.2, f32[4,512]{1,0:T(4,128)S(1)} %fusion.41), kind=kOutput, calls=%fused_computation.21 | convolution fusion | flops 1614282752 | bytes 7348224 | tf_op jit(solution)/shard_map/grf,grd->gfd/dot_general | solution.py:86
  241.8 0.7 select_reduce_fusion
  242.6 14.3 %psum.7 = f32[128,8]{0,1:T(8,128)} all-reduce(f32[128,8]{0,1:T(8,128)S(1)} %select_reduce_fusion), channel_id=1, replica_groups=mesh['dp'=8,'expert'=4] {'dp'}, use_global_device_ids=true, to_apply=%region_8.9 | all-reduce | flops 1024 | bytes 8192 | tf_op jit(solution)/shard_map/psum | solution.py:113
  256.9 1.0 reduce-scatter.10.cloned.1.call-done
  257.9 1.7 fusion.43
  (21 shorter events, 0.1 us)
Async XLA Ops:
  7.2 43.7 %copy-start = (bf16[4,512,768]{2,1,0:T(8,128)(2,1)S(1)}, bf16[4,512,768]{2,1,0:T(8,128)(2,1)}, u32[]{:S(2)}) copy-start(bf16[4,512,768]{2,1,0:T(8,128)(2,1)} %param.11) | copy-start | bytes 9437188
  7.2 41.5 %all-gather.3.cloned.1.call-start = ((), (), s32[]{:S(2)}) async-start(), calls=%async_computation.3 | async-start | bytes 1474560 | tf_op jit(solution)/shard_map/all_gather | solution.py:58
  13.3 0.7 copy-start.3
  14.1 122.7 %reduce-scatter.6.cloned.1.call-start = ((), (), s32[]{:S(2)}) async-start(), calls=%async_computation.4 | async-start | bytes 10616832 | tf_op jit(solution)/shard_map/reduce_scatter | solution.py:33
  50.9 1.9 copy-start.4
  50.9 4.4 %copy-start.1 = (f32[512,512]{0,1:T(8,128)}, f32[512,512]{0,1:T(8,128)S(1)}, u32[]{:S(2)}) copy-start(f32[512,512]{0,1:T(8,128)S(1)} %get-tuple-element.30) | copy-start | bytes 3145732
  50.9 2.5 copy-start.9
  53.3 1.9 copy-start.8
  61.8 137.0 %all-gather.5.cloned.1.call-start = ((), (), s32[]{:S(2)}) async-start(), calls=%async_computation.5 | async-start | bytes 10616832 | tf_op jit(solution)/shard_map/all_gather | solution.py:40
  139.8 102.0 %reduce-scatter.8.cloned.1.call-start = ((), (), s32[]{:S(2)}) async-start(), calls=%async_computation.6 | async-start | bytes 40960 | tf_op jit(solution)/shard_map/reduce_scatter | solution.py:112
  210.6 0.6 copy-start.6
  211.2 46.7 %reduce-scatter.10.cloned.1.call-start = ((), (), s32[]{:S(2)}) async-start(), calls=%async_computation.7 | async-start | bytes 1310720
  224.9 5.6 %copy-start.5 = (bf16[512,512]{0,1:T(8,128)(2,1)S(1)}, bf16[512,512]{0,1:T(8,128)(2,1)}, u32[]{:S(2)}) copy-start(bf16[512,512]{0,1:T(8,128)(2,1)} %copy-done.4) | copy-start | bytes 1572868
  230.5 5.5 %copy-start.2 = (f32[512,512]{0,1:T(8,128)S(1)}, f32[512,512]{0,1:T(8,128)}, u32[]{:S(2)}) copy-start(f32[512,512]{0,1:T(8,128)} %copy-done.1) | copy-start | bytes 3145732
  236.0 5.9 %copy-start.7 = (s32[128,8]{0,1:T(8,128)S(1)}, s32[128,8]{0,1:T(8,128)}, u32[]{:S(2)}) copy-start(s32[128,8]{0,1:T(8,128)} %param.8) | copy-start | bytes 12292
Sparse Core Ops, SparseCore 0:
  14.2 34.4 all-gather.2
  62.0 74.7 reduce-scatter.5
  139.9 58.8 all-gather.4
  211.4 18.9 reduce-scatter.7
  232.6 25.2 reduce-scatter.9

commit v2 on v1

--- a/solution.py
+++ b/solution.py
@@ -10,6 +10,23 @@
     mid = rest.astype(jnp.bfloat16)
     low = (rest - mid.astype(jnp.float32)).astype(jnp.bfloat16)
     return high, mid, low
+
+
+def gather_line(block, axis):
+    count = lax.axis_size(axis)
+    me = lax.axis_index(axis)
+    up_pairs = [(i, i + 1) for i in range(count - 1)]
+    down_pairs = [(i + 1, i) for i in range(count - 1)]
+    from_low, from_high = [], []
+    low = high = block
+    for _ in range(count - 1):
+        low = lax.ppermute(low, axis, up_pairs)
+        high = lax.ppermute(high, axis, down_pairs)
+        from_low.append(low)
+        from_high.append(high)
+    line = jnp.concatenate(from_low[::-1] + [block] + from_high, axis=0)
+    rows = block.shape[0]
+    return lax.dynamic_slice_in_dim(line, (count - 1 - me) * rows, count * rows, 0)
 
 
 def exchange(x_rows, g_rows, probs, w_gate, w_up, w_down):
@@ -55,7 +72,7 @@
     packed = jnp.concatenate(
         [tokens, grad_out, *split_bf16(prob_of), jnp.zeros((tok_rows, pad), jnp.bfloat16)], axis=1
     )
-    gathered = lax.all_gather(packed, "expert", axis=0, tiled=True)
+    gathered = gather_line(packed, "expert")
     count = gathered.shape[0]
     x_all = gathered[:, :width]
     g_all = gathered[:, width : 2 * width]

time: 267 us -> 270 us (1.011)
  starting transfers between devices: 0.39 us -> 19.3 us
  matrix products: 41.4 us -> 32.3 us
  waiting for transfers between devices: 170 us -> 164 us
    all_gather x1 -> x0, waiting for transfers between devices: 34.6 us -> none  [on_device(): gathered = lax.all_gather(packed, 'expert', axis=0, tiled=True)]
    ppermute x0 -> x6, starting transfers between devices: none -> 19 us  [the longest x3 15.1 us: gather_line(): low = lax.ppermute(low, axis, up_pairs)]
    unnamed x6 -> x5, waiting for transfers between devices: 1.13 us -> 14.1 us
    ppermute x0 -> x6, waiting for transfers between devices: none -> 11.6 us  [the longest x3 11.6 us: gather_line(): low = lax.ppermute(low, axis, up_pairs)]
    dot_general x6, matrix products: 35.6 us -> 26.4 us  [dot(): return jnp.einsum(spec, a, b, preferred_element_type=jnp.float32)]
    reduce_scatter x1, waiting for transfers between devices: 74.9 us -> 78.5 us  [exchange(): lax.psum_scatter(part, 'dp', scatter_dimension=0, tiled=True)]
    unnamed x25 -> x43, local copies, waits for them, and re-layouts: 9.5 us -> 13.1 us
  transfers between devices with their start and end apart: 5 -> 10, of which waited for: 4 -> 7; matrix products, arithmetic and copies ran while one was open for 12% -> 9% of each run, Pallas kernels for 0% -> 0%
where the time goes in v2:
time: 270 us; the launch traced here: 269 us
  waiting for transfers between devices  164 us (61%)
  matrix products  32.3 us (12%)
  starting transfers between devices  19.3 us (7%)
  local copies, waits for them, and re-layouts  15.7 us (6%)
  between operations  14.1 us (5%)
  blocking collectives  12.9 us (5%)
  other arithmetic  10.9 us (4%)
    reduce_scatter x1, waiting for transfers between devices, exchange(): lax.psum_scatter(part, 'dp', scatter_dimension=0, tiled=True)  78.5 us
    all_gather x1, waiting for transfers between devices, exchange(): lax.all_gather(act, 'dp', axis=0, tiled=True)  58.7 us
    dot_general x6, matrix products, dot(): return jnp.einsum(spec, a, b, preferred_element_type=jnp.float32)  26.4 us
    ppermute x3, starting transfers between devices, gather_line(): low = lax.ppermute(low, axis, up_pairs)  15.1 us
    unnamed x5, waiting for transfers between devices  14.1 us
    unnamed x43, local copies, waits for them, and re-layouts  13.1 us
    psum x1, blocking collectives, on_device(): lax.psum(jnp.sum(jnp.where(picked, wide[:, None, :], 0.0), axis=2), 'dp')  12.9 us
    ppermute x3, waiting for transfers between devices, gather_line(): low = lax.ppermute(low, axis, up_pairs)  11.6 us
  transfers between devices with their start and end apart: 10, of which 7 were waited for; matrix products, arithmetic and copies ran while one was open for 9% of the time, Pallas kernels for 0%

profile of v2, /device:TPU:0, one launch (start us, length us, event | category | flops | bytes accessed | tf_op | source)
XLA Modules:
  0.0 269.0 jit_solution(11732299047842935092)
XLA Ops:
  7.2 1.2 copy.63
  8.4 0.7 constant_dynamic-update-slice_fusion.5
  9.1 1.0 copy.64
  10.1 0.7 constant_dynamic-update-slice_fusion.4
  10.8 0.7 select_reduce_fusion.1
  11.5 0.6 constant_dynamic-update-slice_fusion.3
  12.1 0.6 constant_dynamic-update-slice_fusion.2
  12.7 0.6 constant_dynamic-update-slice_fusion.1
  13.3 0.6 constant_dynamic-update-slice_fusion
  13.9 4.9 %collective-permute-start = (bf16[128,1152]{0,1:T(8,128)(2,1)}, bf16[128,1152]{0,1:T(8,128)(2,1)S(1)}, u32[]{:S(2)}, u32[]{:S(2)}) collective-permute-start(bf16[128,1152]{0,1:T(8,128)(2,1)} %constant_dynamic-update-slice_fusion), channel_id=1, source_target_pairs={{0,1},{1,2},{2,3},{4,5},{5,6},{6,7},{8,9},{9,10},{10,11},{12,13},{... | collective-permute-start | bytes 884744 | tf_op jit(solution)/shard_map/ppermute | solution.py:23
  18.8 1.3 collective-permute-start.3
  20.1 5.2 %collective-permute-done = bf16[128,1152]{0,1:T(8,128)(2,1)S(1)} collective-permute-done((bf16[128,1152]{0,1:T(8,128)(2,1)}, bf16[128,1152]{0,1:T(8,128)(2,1)S(1)}, u32[]{:S(2)}, u32[]{:S(2)}) %collective-permute-start) | collective-permute-done | bytes 294944 | tf_op jit(solution)/shard_map/ppermute | solution.py:23
  25.4 0.7 copy-done.8
  26.1 5.0 %collective-permute-start.1 = (bf16[128,1152]{0,1:T(8,128)(2,1)S(1)}, bf16[128,1152]{0,1:T(8,128)(2,1)}, u32[]{:S(2)}, u32[]{:S(2)}) collective-permute-start(bf16[128,1152]{0,1:T(8,128)(2,1)S(1)} %collective-permute-done), channel_id=1, source_target_pairs={{0,1},{1,2},{2,3},{4,5},{5,6},{6,7},{8,9},{9,10},{10,11},{12,13},{... | collective-permute-start | bytes 884744 | tf_op jit(solution)/shard_map/ppermute | solution.py:23
  31.1 1.3 collective-permute-start.4
  32.4 3.5 %collective-permute-done.1 = bf16[128,1152]{0,1:T(8,128)(2,1)} collective-permute-done((bf16[128,1152]{0,1:T(8,128)(2,1)S(1)}, bf16[128,1152]{0,1:T(8,128)(2,1)}, u32[]{:S(2)}, u32[]{:S(2)}) %collective-permute-start.1) | collective-permute-done | bytes 294944 | tf_op jit(solution)/shard_map/ppermute | solution.py:23
  35.9 5.2 %collective-permute-start.2 = (bf16[128,1152]{0,1:T(8,128)(2,1)}, bf16[128,1152]{0,1:T(8,128)(2,1)}, u32[]{:S(2)}, u32[]{:S(2)}) collective-permute-start(bf16[128,1152]{0,1:T(8,128)(2,1)} %collective-permute-done.1), channel_id=1, source_target_pairs={{0,1},{1,2},{2,3},{4,5},{5,6},{6,7},{8,9},{9,10},{10,11},{12,13},{... | collective-permute-start | bytes 884744 | tf_op jit(solution)/shard_map/ppermute | solution.py:23
  41.1 1.3 collective-permute-start.5
  42.4 2.9 %collective-permute-done.2 = bf16[128,1152]{0,1:T(8,128)(2,1)} collective-permute-done((bf16[128,1152]{0,1:T(8,128)(2,1)}, bf16[128,1152]{0,1:T(8,128)(2,1)}, u32[]{:S(2)}, u32[]{:S(2)}) %collective-permute-start.2) | collective-permute-done | bytes 294944 | tf_op jit(solution)/shard_map/ppermute | solution.py:23
  45.2 1.0 constant_dynamic-update-slice_fusion.12
  46.2 1.0 constant_dynamic-update-slice_fusion.11
  47.3 1.0 constant_dynamic-update-slice_fusion.10
  48.4 1.0 constant_dynamic-update-slice_fusion.8
  49.5 1.0 constant_dynamic-update-slice_fusion.7
  50.9 1.8 convolution_convert_fusion
  52.7 0.5 copy-done.13
  53.3 1.9 convolution_convert_fusion.1
  55.2 2.2 fusion.15
  57.3 4.4 %pad_maximum_fusion = bf16[4,512,2304]{2,1,0:T(8,128)(2,1)} fusion(bf16[4,512,768]{2,1,0:T(8,128)(2,1)S(1)} %fusion.15, bf16[4,512,768]{2,1,0:T(8,128)(2,1)S(1)} %convolution_convert_fusion, bf16[4,512,768]{2,1,0:T(8,128)(2,1)S(1)} %convolution_convert_fusion.1), kind=kLoop, calls=%fused_computation | loop fusion | flops 28311552 | bytes 18874368 | tf_op jit(solution)/shard_map/concatenate | solution.py:42
  61.8 78.5 %reduce-scatter.6.cloned.1.call-done = bf16[256,2304]{1,0:T(8,128)(2,1)} async-done(((bf16[2048,2304]{1,0:T(8,128)(2,1)}), bf16[256,2304]{1,0:T(8,128)(2,1)}) %reduce-scatter.6.cloned.1.call-update) | async-done | bytes 1179664 | tf_op jit(solution)/shard_map/reduce_scatter | solution.py:50
  140.3 1.4 convert_element_type.69
  141.7 0.5 multiply_convert_fusion.9
  142.2 1.1 pad_maximum_fusion.1
  143.6 58.7 %all-gather.2.cloned.1.call-done = bf16[2048,2304]{1,0:T(8,128)(2,1)} async-done(((bf16[256,2304]{1,0:T(8,128)(2,1)}), bf16[2048,2304]{1,0:T(8,128)(2,1)}) %all-gather.2.cloned.1.call-update) | async-done | bytes 9437200 | tf_op jit(solution)/shard_map/all_gather | solution.py:57
  202.3 3.9 %fusion.6 = f32[4,512,512]{2,1,0:T(8,128)S(1)} fusion(bf16[4,512,768]{2,1,0:T(8,128)(2,1)S(1)} %copy-done, bf16[4,512,2304]{2,1,0:T(8,128)(2,1)} %bitcast.24), kind=kOutput, calls=%fused_computation.11 | convolution fusion | flops 1610612736 | bytes 10485760 | tf_op jit(solution)/shard_map/grf,gdf->grd/dot_general | solution.py:103
  206.2 1.1 copy-done.11
  207.3 4.0 %fusion.1 = (f32[4,512]{1,0:T(4,128)S(1)}, bf16[512,512]{0,1:T(8,128)(2,1)S(1)}) fusion(f32[512,512]{0,1:T(8,128)S(1)} %copy-done.3, f32[4,512]{1,0:T(4,128)S(1)} %fusion.41, bf16[4,768,512]{2,1,0:T(8,128)(2,1)} %param.12, bf16[4,512,2304]{2,1,0:T(8,128)(2,1)S(1)} %bitcast.28), kind=kOutput, calls=%fused_computation.4 | convolution fusion | flops 1616640000 | bytes 7880704 | tf_op jit(solution)/shard_map/grf,gfd->grd/dot_general | solution.py:103
  211.3 1.8 fusion.25
  213.5 0.6 copy-done.9
  214.2 1.3 copy.80
  215.6 5.4 %fusion.19 = bf16[4,512,768]{2,1,0:T(8,128)(2,1)} fusion(bf16[4,512,2304]{2,1,0:T(8,128)(2,1)} %bitcast.25, bf16[512,512]{0,1:T(8,128)(2,1)S(1)} %copy-done.6), kind=kOutput, calls=%fused_computation.22 | convolution fusion | flops 1612185600 | bytes 6815744 | tf_op jit(solution)/shard_map/grd,grf->gdf/dot_general | solution.py:103
  221.0 5.5 %fusion.22 = bf16[4,512,768]{2,1,0:T(8,128)(2,1)} fusion(bf16[4,512,2304]{2,1,0:T(8,128)(2,1)} %bitcast.26, bf16[512,512]{0,1:T(8,128)(2,1)S(1)} %copy-done.7), kind=kOutput, calls=%fused_computation.23 | convolution fusion | flops 1612185600 | bytes 6815744 | tf_op jit(solution)/shard_map/grd,grf->gdf/dot_general | solution.py:103
  226.5 5.8 %fusion.16 = bf16[4,768,512]{2,1,0:T(8,128)(2,1)} fusion(bf16[4,512,2304]{2,1,0:T(8,128)(2,1)} %bitcast.27, f32[512,512]{0,1:T(8,128)S(1)} %copy-done.4, f32[4,512]{1,0:T(4,128)S(1)} %fusion.41), kind=kOutput, calls=%fused_computation.21 | convolution fusion | flops 1614282752 | bytes 7348224 | tf_op jit(solution)/shard_map/grf,grd->gfd/dot_general | solution.py:103
  232.3 0.9 reduce-scatter.8.cloned.1.call-done
  233.1 0.7 select_reduce_fusion
  233.9 12.9 %psum.7 = f32[128,8]{0,1:T(8,128)} all-reduce(f32[128,8]{0,1:T(8,128)S(1)} %select_reduce_fusion), channel_id=1, replica_groups=mesh['dp'=8,'expert'=4] {'dp'}, use_global_device_ids=true, to_apply=%region_8.9 | all-reduce | flops 1024 | bytes 8192 | tf_op jit(solution)/shard_map/psum | solution.py:130
  246.7 14.0 %reduce-scatter.10.cloned.1.call-done = bf16[128,1024]{1,0:T(8,128)(2,1)} async-done(((bf16[512,1024]{1,0:T(8,128)(2,1)}), bf16[128,1024]{1,0:T(8,128)(2,1)}) %reduce-scatter.10.cloned.1.call-update) | async-done | bytes 262160
  260.7 1.7 fusion.42
  (52 shorter events, 1.2 us)
Async XLA Ops:
  7.2 43.7 %copy-start = (bf16[4,512,768]{2,1,0:T(8,128)(2,1)S(1)}, bf16[4,512,768]{2,1,0:T(8,128)(2,1)}, u32[]{:S(2)}) copy-start(bf16[4,512,768]{2,1,0:T(8,128)(2,1)} %param.11) | copy-start | bytes 9437188
  7.2 133.1 %reduce-scatter.6.cloned.1.call-start = ((), (), s32[]{:S(2)}) async-start(), calls=%async_computation.3 | async-start | bytes 10616832 | tf_op jit(solution)/shard_map/reduce_scatter | solution.py:50
  13.9 11.5 %collective-permute-start = (bf16[128,1152]{0,1:T(8,128)(2,1)}, bf16[128,1152]{0,1:T(8,128)(2,1)S(1)}, u32[]{:S(2)}, u32[]{:S(2)}) collective-permute-start(bf16[128,1152]{0,1:T(8,128)(2,1)} %constant_dynamic-update-slice_fusion), channel_id=1, source_target_pairs={{0,1},{1,2},{2,3},{4,5},{5,6},{6,7},{8,9},{9,10},{10,11},{12,13},{... | collective-permute-start | bytes 884744 | tf_op jit(solution)/shard_map/ppermute | solution.py:23
  18.8 12.3 %collective-permute-start.3 = (bf16[128,1152]{0,1:T(8,128)(2,1)}, bf16[128,1152]{0,1:T(8,128)(2,1)}, u32[]{:S(2)}, u32[]{:S(2)}) collective-permute-start(bf16[128,1152]{0,1:T(8,128)(2,1)} %constant_dynamic-update-slice_fusion), channel_id=1, source_target_pairs={{1,0},{2,1},{3,2},{5,4},{6,5},{7,6},{9,8},{10,9},{11,10},{13,12},{... | collective-permute-start | bytes 884744 | tf_op jit(solution)/shard_map/ppermute | solution.py:24
  25.4 0.7 copy-start.8
  26.1 9.8 %collective-permute-start.1 = (bf16[128,1152]{0,1:T(8,128)(2,1)S(1)}, bf16[128,1152]{0,1:T(8,128)(2,1)}, u32[]{:S(2)}, u32[]{:S(2)}) collective-permute-start(bf16[128,1152]{0,1:T(8,128)(2,1)S(1)} %collective-permute-done), channel_id=1, source_target_pairs={{0,1},{1,2},{2,3},{4,5},{5,6},{6,7},{8,9},{9,10},{10,11},{12,13},{... | collective-permute-start | bytes 884744 | tf_op jit(solution)/shard_map/ppermute | solution.py:23
  31.1 10.0 %collective-permute-start.4 = (bf16[128,1152]{0,1:T(8,128)(2,1)}, bf16[128,1152]{0,1:T(8,128)(2,1)}, u32[]{:S(2)}, u32[]{:S(2)}) collective-permute-start(bf16[128,1152]{0,1:T(8,128)(2,1)} %collective-permute-done.3), channel_id=1, source_target_pairs={{1,0},{2,1},{3,2},{5,4},{6,5},{7,6},{9,8},{10,9},{11,10},{13,12},{... | collective-permute-start | bytes 884744 | tf_op jit(solution)/shard_map/ppermute | solution.py:24
  35.9 9.4 %collective-permute-start.2 = (bf16[128,1152]{0,1:T(8,128)(2,1)}, bf16[128,1152]{0,1:T(8,128)(2,1)}, u32[]{:S(2)}, u32[]{:S(2)}) collective-permute-start(bf16[128,1152]{0,1:T(8,128)(2,1)} %collective-permute-done.1), channel_id=1, source_target_pairs={{0,1},{1,2},{2,3},{4,5},{5,6},{6,7},{8,9},{9,10},{10,11},{12,13},{... | collective-permute-start | bytes 884744 | tf_op jit(solution)/shard_map/ppermute | solution.py:23
  41.1 9.5 %collective-permute-start.5 = (bf16[128,1152]{0,1:T(8,128)(2,1)}, bf16[128,1152]{0,1:T(8,128)(2,1)S(1)}, u32[]{:S(2)}, u32[]{:S(2)}) collective-permute-start(bf16[128,1152]{0,1:T(8,128)(2,1)} %collective-permute-done.4), channel_id=1, source_target_pairs={{1,0},{2,1},{3,2},{5,4},{6,5},{7,6},{9,8},{10,9},{11,10},{13,12},{... | collective-permute-start | bytes 884744 | tf_op jit(solution)/shard_map/ppermute | solution.py:24
  50.8 1.9 copy-start.5
  50.8 4.4 %copy-start.2 = (f32[512,512]{0,1:T(8,128)}, f32[512,512]{0,1:T(8,128)S(1)}, u32[]{:S(2)}) copy-start(f32[512,512]{0,1:T(8,128)S(1)} %get-tuple-element.30) | copy-start | bytes 3145732
  50.9 2.4 copy-start.13
  53.3 1.9 copy-start.12
  61.7 140.6 %all-gather.2.cloned.1.call-start = ((), (), s32[]{:S(2)}) async-start(), calls=%async_computation.4 | async-start | bytes 10616832 | tf_op jit(solution)/shard_map/all_gather | solution.py:57
  143.3 89.8 %reduce-scatter.8.cloned.1.call-start = ((), (), s32[]{:S(2)}) async-start(), calls=%async_computation.5 | async-start | bytes 40960 | tf_op jit(solution)/shard_map/reduce_scatter | solution.py:129
  202.3 3.9 %copy-start.3 = (f32[512,512]{0,1:T(8,128)S(1)}, f32[512,512]{0,1:T(8,128)}, u32[]{:S(2)}) copy-start(f32[512,512]{0,1:T(8,128)} %copy-done.2) | copy-start | bytes 3145732
  202.3 5.0 %copy-start.11 = (bf16[2048,2304]{1,0:T(8,128)(2,1)S(1)}, bf16[2048,2304]{1,0:T(8,128)(2,1)}, u32[]{:S(2)}) copy-start(bf16[2048,2304]{1,0:T(8,128)(2,1)} %all-gather.2.cloned.1.call-done) | copy-start | bytes 28311556
  207.3 4.0 %copy-start.14 = (bf16[4,512,768]{2,1,0:T(8,128)(2,1)S(1)}, bf16[4,512,768]{2,1,0:T(8,128)(2,1)}, u32[]{:S(2)}) copy-start(bf16[4,512,768]{2,1,0:T(8,128)(2,1)} %param.10) | copy-start | bytes 9437188
  213.2 2.4 copy-start.6
  213.5 0.6 copy-start.9
  214.1 46.6 %reduce-scatter.10.cloned.1.call-start = ((), (), s32[]{:S(2)}) async-start(), calls=%async_computation.6 | async-start | bytes 1310720
  215.6 5.4 %copy-start.7 = (bf16[512,512]{0,1:T(8,128)(2,1)S(1)}, bf16[512,512]{0,1:T(8,128)(2,1)}, u32[]{:S(2)}) copy-start(bf16[512,512]{0,1:T(8,128)(2,1)} %copy-done.5) | copy-start | bytes 1572868
  221.0 5.5 %copy-start.4 = (f32[512,512]{0,1:T(8,128)S(1)}, f32[512,512]{0,1:T(8,128)}, u32[]{:S(2)}) copy-start(f32[512,512]{0,1:T(8,128)} %copy-done.2) | copy-start | bytes 3145732
  221.0 41.4 %copy-start.1 = (bf16[4,512,768]{2,1,0:T(8,128)(2,1)S(1)}, bf16[4,512,768]{2,1,0:T(8,128)(2,1)}, u32[]{:S(2)}) copy-start(bf16[4,512,768]{2,1,0:T(8,128)(2,1)} %param.11) | copy-start | bytes 9437188
  226.5 6.6 %copy-start.10 = (s32[128,8]{0,1:T(8,128)S(1)}, s32[128,8]{0,1:T(8,128)}, u32[]{:S(2)}) copy-start(s32[128,8]{0,1:T(8,128)} %param.8) | copy-start | bytes 12292
Sparse Core Ops, SparseCore 0:
  61.8 78.4 reduce-scatter.5
  143.5 58.8 all-gather.1
  214.2 18.8 reduce-scatter.7
  235.4 25.3 reduce-scatter.9
